TPU v7x, 256 devices: a whole 4x4x8 slice. The times are simulated.
256 devices in a mesh: dp: 16 (over z_hi, x), expert: 16 (over y, z_lo, core).
Axes of the slice: x: 4, y: 4, z: 8 (z_hi: 4, z_lo: 2; z = z_hi * 2 + z_lo), core: 2. Of those that a mesh axis runs over, the one named last changes fastest.
Arguments:
- tokens: bfloat16 [2048, 3072], P('dp'), may hold values from -6 to 6
- cotangent: bfloat16 [2048, 3072], P('dp'), may hold values from -6 to 6
- routes: int32 [2048, 4], P('dp'), may hold values from 0 to 15, all different within a row; in each aligned block of 128 rows (0 to 127, 128 to 255, ...) at most 48 rows name the same one
- route_weights: float32 [2048, 4], P('dp'), may hold values from 0.1 to 0.6
- gate_weight: bfloat16 [16, 3072, 6144], P('expert', None, 'dp'), may hold values from -0.109375 to 0.109375
- down_weight: bfloat16 [16, 6144, 3072], P('expert', 'dp'), may hold values from -0.078125 to 0.078125
Outputs:
- mixed: bfloat16 [2048, 3072], P('dp')
- token_grad: bfloat16 [2048, 3072], P('dp')
- gate_grad: bfloat16 [16, 3072, 6144], P('expert', None, 'dp')
- down_grad: bfloat16 [16, 6144, 3072], P('expert', 'dp')
Inputs may be any that keep to these rules, and one draw needn't show every extreme that they name: `routes`: each row names 4 different experts. In each aligned block of 128 rows no expert is named by more than 48 rows, and in every draw some expert is named by exactly 48 rows of some block.
All inputs are finite; a program needn't handle non-finite values.
Results may differ from a plain program's by a relative error of at most 0.022.
Values may be sent and summed in bfloat16 or wider, within the bound.
A program may use at most 128 MiB of HBM per device.

v0:
```python
import jax
import jax.numpy as jnp
from jax import lax
from jax.sharding import PartitionSpec as P

CAP = 48


def shards(tokens, cotangent, routes, route_weights, gate_weight, down_weight):
    local = gate_weight.shape[0]
    first_expert = lax.axis_index("expert") * local
    expert_ids = first_expert + jnp.arange(local, dtype=jnp.int32)
    matches = routes[None, :, :] == expert_ids[:, None, None]
    member = jnp.any(matches, axis=2)
    weight_sum = jnp.sum(jnp.where(matches, route_weights[None, :, :], 0.0), axis=2)
    position = jnp.cumsum(member.astype(jnp.int32), axis=1) - 1
    slots = jnp.arange(CAP, dtype=jnp.int32)
    selector = (member[None, :, :] & (position[None, :, :] == slots[:, None, None])).astype(
        jnp.float32
    )
    select_half = selector.astype(jnp.bfloat16)
    row_scale = jnp.einsum("clt,lt->cl", selector, weight_sum, precision=lax.Precision.HIGHEST)
    token_sel = jnp.einsum(
        "clt,td->cld", select_half, tokens, preferred_element_type=jnp.float32
    ).astype(jnp.bfloat16)
    grad_sel = jnp.einsum("clt,td->cld", select_half, cotangent, preferred_element_type=jnp.float32)
    grad_sel = (grad_sel * row_scale[:, :, None]).astype(jnp.bfloat16)
    token_rows = lax.all_gather(token_sel, "dp", axis=0, tiled=True)
    pre_act = jnp.einsum(
        "rld,ldf->rlf", token_rows, gate_weight, preferred_element_type=jnp.float32
    )
    act_rows = jax.nn.silu(pre_act).astype(jnp.bfloat16)
    piece = act_rows
    expert_out = lax.psum_scatter(
        jnp.einsum("rlf,lfd->rld", piece, down_weight, preferred_element_type=jnp.float32).astype(
            jnp.bfloat16
        ),
        "dp",
        scatter_dimension=0,
        tiled=True,
    ).astype(jnp.float32)
    token_out = jnp.einsum(
        "clt,cld->td", selector, expert_out * row_scale[:, :, None], precision=lax.Precision.HIGHEST
    )
    mixed = lax.psum(token_out.astype(jnp.bfloat16), "expert")
    grad_rows = lax.all_gather(grad_sel, "dp", axis=0, tiled=True)
    back_act = jnp.einsum(
        "rld,lfd->rlf", grad_rows, down_weight, preferred_element_type=jnp.float32
    )
    sigma = jax.nn.sigmoid(pre_act)
    grad_pre = (back_act * sigma * (1.0 + pre_act * (1.0 - sigma))).astype(jnp.bfloat16)
    down_grad = jnp.einsum(
        "rlf,rld->lfd", act_rows, grad_rows, preferred_element_type=jnp.float32
    ).astype(jnp.bfloat16)
    gate_grad = jnp.einsum(
        "rld,rlf->ldf", token_rows, grad_pre, preferred_element_type=jnp.float32
    ).astype(jnp.bfloat16)
    piece = grad_pre
    expert_back = lax.psum_scatter(
        jnp.einsum("rlf,ldf->rld", piece, gate_weight, preferred_element_type=jnp.float32).astype(
            jnp.bfloat16
        ),
        "dp",
        scatter_dimension=0,
        tiled=True,
    ).astype(jnp.float32)
    token_back = jnp.einsum("clt,cld->td", selector, expert_back, precision=lax.Precision.HIGHEST)
    token_grad = lax.psum(token_back.astype(jnp.bfloat16), "expert")
    return (mixed, token_grad, gate_grad, down_grad)


def solution(mesh):
    return jax.shard_map(
        shards,
        mesh=mesh,
        in_specs=(
            P("dp", None),
            P("dp", None),
            P("dp", None),
            P("dp", None),
            P("expert", None, "dp"),
            P("expert", "dp", None),
        ),
        out_specs=(P("dp", None), P("dp", None), P("expert", None, "dp"), P("expert", "dp", None)),
        check_vma=False,
    )
```

profile of v0, /device:TPU:1, one launch (start us, length us, event | category | flops | bytes accessed | tf_op | source)
XLA Modules:
  0.0 521.7 jit_solution(7524219493285349250)
XLA Ops:
  7.2 0.0 all-gather.5.cloned.1.call-start
  7.2 0.9 select_reduce_fusion
  8.1 0.1 copy.11
  8.2 0.2 reduce-window.7
  8.4 0.1 add_reduce_fusion
  8.5 2.1 convolution_convert_fusion.6
  10.6 0.0 all-gather.5.cloned.1.call-update
  10.7 0.0 all-gather.7.cloned.1.call-start
  10.7 0.1 convolution_bitcast_fusion
  10.8 2.1 fusion.4
  13.0 0.0 all-gather.7.cloned.1.call-update
  13.0 0.0 reduce-scatter.3.cloned.1.call-start
  13.0 84.5 %all-gather.5.cloned.1.call-done = bf16[768,3072]{1,0:T(8,128)(2,1)} async-done(((bf16[48,3072]{1,0:T(8,128)(2,1)}), bf16[768,3072]{1,0:T(8,128)(2,1)}) %all-gather.5.cloned.1.call-update) | async-done | bytes 4718608 | tf_op jit(solution)/shard_map/all_gather | solution.py:28
  97.5 5.2 fusion.11
  102.7 4.3 fusion
  107.0 0.0 reduce-scatter.3.cloned.1.call-update
  107.0 0.0 reduce-scatter.5.cloned.1.call-start
  107.1 74.3 %all-gather.7.cloned.1.call-done = bf16[768,3072]{1,0:T(8,128)(2,1)} async-done(((bf16[48,3072]{1,0:T(8,128)(2,1)}), bf16[768,3072]{1,0:T(8,128)(2,1)}) %all-gather.7.cloned.1.call-update) | async-done | bytes 4718608 | tf_op jit(solution)/shard_map/all_gather | solution.py:46
  181.4 5.3 %fusion.26 = bf16[768,384]{1,0:T(8,128)(2,1)S(1)} fusion(bf16[768,3072]{1,0:T(8,128)(2,1)} %all-gather.7.cloned.1.call-done, bf16[1,384,3072]{2,1,0:T(8,128)(2,1)S(1)} %copy-done, f32[768,1,384]{2,0,1:T(8,128)S(1)} %fusion.11), kind=kOutput, calls=%fused_computation.24 | convolution fusion | flops 1814593536 | bytes 8847360 | tf_op jit(solution)/shard_map/rld,lfd->rlf/dot_general | solution.py:47
  186.7 0.8 copy-done.4
  187.5 4.3 fusion.1
  191.8 0.0 reduce-scatter.5.cloned.1.call-update
  191.8 0.0 all-reduce.3.cloned.1.call-start
  191.9 90.0 %reduce-scatter.3.cloned.1.call-done = bf16[48,1,3072]{2,0,1:T(8,128)(2,1)} async-done(((bf16[768,1,3072]{2,0,1:T(8,128)(2,1)}), bf16[48,1,3072]{2,0,1:T(8,128)(2,1)}) %reduce-scatter.3.cloned.1.call-update) | async-done | bytes 294928 | tf_op jit(solution)/shard_map/reduce_scatter | solution.py:34
  281.8 2.7 convolution_convert_fusion.5
  284.5 98.3 %reduce-scatter.5.cloned.1.call-done = bf16[48,1,3072]{2,0,1:T(8,128)(2,1)} async-done(((bf16[768,1,3072]{2,0,1:T(8,128)(2,1)}), bf16[48,1,3072]{2,0,1:T(8,128)(2,1)}) %reduce-scatter.5.cloned.1.call-update) | async-done | bytes 294928 | tf_op jit(solution)/shard_map/reduce_scatter | solution.py:59
  382.8 2.3 convolution_convert_fusion.4
  385.1 6.6 %fusion.2 = bf16[1,3072,384]{2,1,0:T(8,128)(2,1)} fusion(bf16[768,3072]{1,0:T(8,128)(2,1)} %all-gather.5.cloned.1.call-done, bf16[768,384]{1,0:T(8,128)(2,1)S(1)} %copy-done.5), kind=kOutput, calls=%fused_computation.6 | convolution fusion | flops 1813118976 | bytes 7667712 | tf_op jit(solution)/shard_map/rld,rlf->ldf/dot_general | solution.py:55
  391.7 3.6 fusion.3
  395.3 115.8 %all-reduce.3.cloned.1.call-done = (bf16[128,3072]{1,0:T(8,128)(2,1)}, bf16[128,3072]{1,0:T(8,128)(2,1)}) async-done(((bf16[128,3072]{1,0:T(8,128)(2,1)}, bf16[128,3072]{1,0:T(8,128)(2,1)}), (bf16[128,3072]{1,0:T(8,128)(2,1)}, bf16[128,3072]{1,0:T(8,128)(2,1)})) %all-reduce.3.cloned.1.call-update) | async-done | bytes 1572880 | tf_op jit(solution)/shard_map/psum | solution.py:45
  511.1 2.1 copy.14
  513.1 2.1 copy.15
  (19 shorter events, 0.1 us)
Async XLA Ops:
  7.2 95.5 %copy-start = (bf16[1,384,3072]{2,1,0:T(8,128)(2,1)S(1)}, bf16[1,384,3072]{2,1,0:T(8,128)(2,1)}, u32[]{:S(2)}) copy-start(bf16[1,384,3072]{2,1,0:T(8,128)(2,1)} %param.11) | copy-start | bytes 7077892
  7.2 90.3 %all-gather.5.cloned.1.call-start = ((), (), s32[]{:S(2)}) async-start(), calls=%async_computation.4 | async-start | bytes 5013504 | tf_op jit(solution)/shard_map/all_gather | solution.py:28
  10.7 170.7 %all-gather.7.cloned.1.call-start = ((), (), s32[]{:S(2)}) async-start(), calls=%async_computation.5 | async-start | bytes 5013504 | tf_op jit(solution)/shard_map/all_gather | solution.py:46
  13.0 268.9 %reduce-scatter.3.cloned.1.call-start = ((), (), s32[]{:S(2)}) async-start(), calls=%async_computation.2 | async-start | bytes 5013504 | tf_op jit(solution)/shard_map/reduce_scatter | solution.py:34
  102.7 78.7 %copy-start.2 = (f32[768,1,384]{2,0,1:T(8,128)}, f32[768,1,384]{2,0,1:T(8,128)S(1)}, u32[]{:S(2)}) copy-start(f32[768,1,384]{2,0,1:T(8,128)S(1)} %fusion.11) | copy-start | bytes 3538948
  107.0 275.8 %reduce-scatter.5.cloned.1.call-start = ((), (), s32[]{:S(2)}) async-start(), calls=%async_computation.3 | async-start | bytes 5013504 | tf_op jit(solution)/shard_map/reduce_scatter | solution.py:59
  181.4 6.1 %copy-start.1 = (bf16[1,3072,384]{2,1,0:T(8,128)(2,1)S(1)}, bf16[1,3072,384]{2,1,0:T(8,128)(2,1)}, u32[]{:S(2)}) copy-start(bf16[1,3072,384]{2,1,0:T(8,128)(2,1)} %param.10) | copy-start | bytes 7077892
  186.6 0.8 copy-start.4
  191.8 193.3 %copy-start.5 = (bf16[768,384]{1,0:T(8,128)(2,1)S(1)}, bf16[768,384]{1,0:T(8,128)(2,1)}, u32[]{:S(2)}) copy-start(bf16[768,384]{1,0:T(8,128)(2,1)} %copy-done.4) | copy-start | bytes 1769476
  191.8 319.2 %all-reduce.3.cloned.1.call-start = ((), (), s32[]{:S(2)}) async-start(), calls=%async_computation.6 | async-start | bytes 3145728 | tf_op jit(solution)/shard_map/psum | solution.py:45
  385.1 6.6 %slice-start = ((s8[4718592]{0:T(1024)(128)(4,1)}), s8[524288]{0:T(1024)(128)(4,1)S(1)}, s32[]{:S(2)}) async-start(s8[4718592]{0:T(1024)(128)(4,1)} %bitcast.90), calls=%async_computation.7 | async-start | bytes 1048576
  385.1 6.6 %slice-start.1 = ((s8[4718592]{0:T(1024)(128)(4,1)}), s8[4194304]{0:T(1024)(128)(4,1)S(1)}, s32[]{:S(2)}) async-start(s8[4718592]{0:T(1024)(128)(4,1)} %bitcast.90), calls=%async_computation.8 | async-start | bytes 8388608
  385.1 6.6 %copy-start.3 = (f32[768,1,384]{2,0,1:T(8,128)S(1)}, f32[768,1,384]{2,0,1:T(8,128)}, u32[]{:S(2)}) copy-start(f32[768,1,384]{2,0,1:T(8,128)} %copy-done.2) | copy-start | bytes 3538948
Sparse Core Ops, SparseCore 0:
  11.0 86.4 all-gather.4
  100.5 80.8 all-gather.6
  185.0 96.7 reduce-scatter.2
  285.3 97.4 reduce-scatter.4
  385.9 125.0 all-reduce.2
where the time goes:
time: 522 us
  waiting for transfers between devices  463 us (89%)
  matrix products  38.5 us (7%)
  between operations  13.9 us (3%)
    psum x1, waiting for transfers between devices, shards(): mixed = lax.psum(token_out.astype(jnp.bfloat16), 'expert')  116 us
    reduce_scatter x1, waiting for transfers between devices, shards(): lax.psum_scatter(jnp.einsum('rlf,ldf->rld', piece, gate_weight, preferred...  98.3 us
    reduce_scatter x1, waiting for transfers between devices, shards(): lax.psum_scatter(jnp.einsum('rlf,lfd->rld', piece, down_weight, preferred...  90 us
    all_gather x1, waiting for transfers between devices, shards(): token_rows = lax.all_gather(token_sel, 'dp', axis=0, tiled=True)  84.5 us
    all_gather x1, waiting for transfers between devices, shards(): grad_rows = lax.all_gather(grad_sel, 'dp', axis=0, tiled=True)  74.3 us
  transfers between devices with their start and end apart: 5, of which 5 were waited for; matrix products, arithmetic and copies ran while one was open for 7% of the time, Pallas kernels for 0%

commit v1 on v0

v1 whole, which is shorter than its diff:
```python
import functools

import jax
import jax.numpy as jnp
from jax import lax
from jax.experimental import pallas as pl
from jax.experimental.pallas import tpu as pltpu
from jax.sharding import PartitionSpec as P

MESH = pl.DeviceIdType.MESH
BF = jnp.bfloat16
F32 = jnp.float32
CAP = 48
TOK = 128
D = 3072
HID = 384
NE = 16
A_COLS = 2432
CHUNKS = ((0, 1024), (1024, 2048), (2048, A_COLS))
NCH = 3
VM = pl.BlockSpec(memory_space=pltpu.VMEM)
HB = pl.BlockSpec(memory_space=pl.ANY)


def kernel(
    tok, cot, routes, wts, gate_in, down_in,
    out, gg_out, dg_out,
    gat, par, rd1, rd2, gate, down, gg, dg, act_s, gp_s, ex, rx, ox, sel_s, scale_s,
    ssem, rsem, xs, xr, os_, or_, lsem,
):
    dp = lax.axis_index("dp")
    me = lax.axis_index("expert")
    h, x = dp // 4, dp % 4
    core, slot = me % 2, me // 2

    def peer(axis, step):
        if axis == "x":
            return (h * 4 + (x + step + 4) % 4, me)
        return (((h + step + 4) % 4) * 4 + x, me)

    load_gate = pltpu.make_async_copy(gate_in, gate, lsem.at[0])
    load_down = pltpu.make_async_copy(down_in, down, lsem.at[1])
    load_gate.start()
    load_down.start()

    barrier = pltpu.get_barrier_semaphore()
    for axis in ("x", "z"):
        for step in (1, -1):
            pl.semaphore_signal(barrier, inc=1, device_id=peer(axis, step), device_id_type=MESH)

    def greet(i, carry):
        pl.semaphore_signal(barrier, inc=1, device_id=(dp, (me + i) % NE), device_id_type=MESH)
        return carry

    lax.fori_loop(1, NE, greet, 0)

    r = routes[...]
    w = wts[...]
    lane16 = lax.broadcasted_iota(jnp.int32, (TOK, NE), 1)
    member = jnp.zeros((TOK, NE), F32)
    for k in range(4):
        member = member + jnp.where(r[:, k : k + 1] == lane16, 1.0, 0.0)
    below = lax.broadcasted_iota(jnp.int32, (TOK, TOK), 0) > lax.broadcasted_iota(
        jnp.int32, (TOK, TOK), 1
    )
    pos = jnp.dot(
        jnp.where(below, 1.0, 0.0).astype(BF), member.astype(BF), preferred_element_type=F32
    )
    mine = jnp.where(lane16 == me, 1.0, 0.0)
    mem_e = jnp.sum(member * mine, axis=1, keepdims=True)
    pos_e = jnp.sum(pos * mine, axis=1, keepdims=True)
    w_e = jnp.zeros((TOK, 1), F32)
    for k in range(4):
        w_e = w_e + jnp.where(r[:, k : k + 1] == me, w[:, k : k + 1], 0.0)
    lane = lax.broadcasted_iota(jnp.int32, (TOK, TOK), 1).astype(F32)
    sel_t = jnp.where((pos_e == lane) & (mem_e > 0.5), 1.0, 0.0)
    sel = sel_t.T[:CAP]
    w_row = jnp.broadcast_to(w_e, (TOK, TOK)).T[:CAP]
    scale_s[...] = jnp.broadcast_to(jnp.sum(sel * w_row, axis=1, keepdims=True), (CAP, 128))
    sel_b = sel.astype(BF)
    gat[0, 0, 0] = jnp.dot(sel_b, tok[...], preferred_element_type=F32).astype(BF)
    scaled = (cot[...].astype(F32) * w_e).astype(BF)
    gat[0, 0, 1] = jnp.dot(sel_b, scaled, preferred_element_type=F32).astype(BF)

    pl.semaphore_wait(barrier, 4 + NE - 1)

    started = []
    count = [0]

    def remote(src, dst, device):
        i = count[0]
        count[0] += 1
        copy = pltpu.make_async_remote_copy(
            src_ref=src, dst_ref=dst, send_sem=ssem.at[i], recv_sem=rsem.at[i],
            device_id=device, device_id_type=MESH,
        )
        return copy

    def go(copy):
        copy.start()
        started.append(copy)

    class Gather:
        def __init__(self, axis, at):
            self.plus, self.minus = peer(axis, 1), peer(axis, -1)
            self.at = at
            self.p, self.m, self.f = {}, {}, {}
            for arr in (0, 1):
                self.p[arr] = remote(at(0, arr), at(3, arr), self.plus)
                self.m[arr] = remote(at(0, arr), at(1, arr), self.minus)
            self.f[0] = remote(at(3, 0), at(2, 0), self.plus)
            self.f[1] = remote(at(1, 1), at(2, 1), self.minus)

        def start(self, arr):
            first, second = (self.p, self.m) if arr == 0 else (self.m, self.p)
            go(first[arr])
            go(second[arr])

        def fwd(self, arr):
            (self.p if arr == 0 else self.m)[arr].wait_recv()
            go(self.f[arr])

        def near(self, arr):
            (self.m if arr == 0 else self.p)[arr].wait_recv()

        def far(self, arr):
            self.f[arr].wait_recv()

    ca, cb = pl.ds(0, A_COLS), pl.ds(A_COLS, D - A_COLS)
    a1 = Gather("z", lambda i, arr: gat.at[i, 0, arr, :, ca])
    b1 = Gather("x", lambda i, arr: gat.at[0, i, arr, :, cb])
    a2 = [Gather("x", functools.partial(lambda u, i, arr: gat.at[u, i, arr, :, ca], u)) for u in range(4)]
    b2 = [Gather("z", functools.partial(lambda u, i, arr: gat.at[i, u, arr, :, cb], u)) for u in range(4)]

    def finish(ring):
        ring.near(0)
        ring.near(1)
        ring.far(0)
        ring.far(1)

    def rows(ref):
        return ref.reshape(4 * CAP, ref.shape[-1])

    def batch(u):
        t = rows(gat[u, :, 0])
        pre = jnp.dot(t, gate[...], preferred_element_type=F32)
        back = lax.dot_general(
            rows(gat[u, :, 1]), down[...], (((1,), (1,)), ((), ())), preferred_element_type=F32
        )
        s = jax.nn.sigmoid(pre)
        act = (pre * s).astype(BF)
        gp = (back * s * (1.0 + pre * (1.0 - s))).astype(BF)
        act_s[u] = act
        gp_s[u] = gp

        def cols(j, carry):
            c = pl.ds(pl.multiple_of(j * 512, 512), 512)
            o = jnp.dot(act_s[u], down[:, c], preferred_element_type=F32).astype(BF)
            par[u, :, 0, :, c] = o.reshape(4, CAP, 512)
            b = lax.dot_general(
                gp_s[u], gate[c, :], (((1,), (1,)), ((), ())), preferred_element_type=F32
            ).astype(BF)
            par[u, :, 1, :, c] = b.reshape(4, CAP, 512)
            return carry

        lax.fori_loop(0, D // 512, cols, 0)

    for arr in (0, 1):
        a1.start(arr)
    for arr in (0, 1):
        b1.start(arr)
    for arr in (0, 1):
        a2[0].start(arr)
        b2[0].start(arr)
    b1.fwd(0)
    b1.fwd(1)
    a2[0].fwd(0)
    a2[0].fwd(1)
    a1.fwd(0)
    a2[3].start(0)
    a1.fwd(1)
    a2[1].start(1)
    b1.near(0)
    b1.near(1)
    for arr in (0, 1):
        b2[1].start(arr)
        b2[3].start(arr)
    load_gate.wait()
    load_down.wait()
    finish(a2[0])
    b1.far(0)
    b1.far(1)
    for arr in (0, 1):
        b2[2].start(arr)
    batch(0)
    a1.near(0)
    a2[1].start(0)
    a1.near(1)
    a2[3].start(1)
    a2[3].fwd(0)
    a2[1].fwd(1)
    b2[0].fwd(0)
    b2[0].fwd(1)
    a1.far(0)
    a2[2].start(0)
    a1.far(1)
    a2[2].start(1)
    a2[1].fwd(0)
    a2[3].fwd(1)
    for u in (1, 3):
        b2[u].fwd(0)
        b2[u].fwd(1)
    b2[2].fwd(0)
    b2[2].fwd(1)
    for u in range(4):
        b2[u].near(0)
        b2[u].near(1)
    finish(a2[1])
    batch(1)
    a2[2].fwd(0)
    a2[2].fwd(1)
    finish(a2[3])
    batch(3)
    for u in range(4):
        b2[u].far(0)
        b2[u].far(1)
    finish(a2[2])
    batch(2)

    class Reduce:
        def __init__(self, axis, at, land, c):
            plus, minus = peer(axis, 1), peer(axis, -1)
            self.at, self.land, self.c = at, land, c
            self.f0 = remote(at(2, 0), land(0, 0), plus)
            self.f1 = remote(at(2, 1), land(0, 1), minus)
            self.l1 = remote(at(1, 1), land(1, 1), plus)
            self.r0 = remote(at(3, 0), land(2, 0), minus)
            self.l0 = remote(at(1, 0), land(1, 0), plus)
            self.r1 = remote(at(3, 1), land(2, 1), minus)

        def start(self):
            go(self.f0)
            go(self.f1)
            go(self.l1)
            go(self.r0)

        def fwd(self):
            for f, copy, i, arr in ((self.f0, self.l0, 1, 0), (self.f1, self.r1, 3, 1)):
                f.wait_recv()
                dst = self.at(i, arr)
                dst[...] = (dst[...].astype(F32) + self.land(0, arr)[...].astype(F32)).astype(BF)
                go(copy)

        def total(self, arr):
            return (
                self.at(0, arr)[...].astype(F32)
                + self.land(1, arr)[...].astype(F32)
                + self.land(2, arr)[...].astype(F32)
            )

        def arrive(self):
            for copy in (self.l1, self.r0, self.l0, self.r1):
                copy.wait_recv()

        def fin(self):
            self.arrive()
            for arr in (0, 1):
                self.at(0, arr)[...] = self.total(arr).astype(BF)

    def stage1(axis, u, c):
        if axis == "x":
            at = lambda i, arr: par.at[u, i, arr, :, c]
        else:
            at = lambda i, arr: par.at[i, u, arr, :, c]
        return Reduce(axis, at, lambda kind, arr: rd1.at[u, kind, arr, :, c], c)

    def stage2(axis, c):
        if axis == "x":
            at = lambda i, arr: par.at[0, i, arr, :, c]
        else:
            at = lambda i, arr: par.at[i, 0, arr, :, c]
        return Reduce(axis, at, lambda kind, arr: rd2.at[kind, arr, :, c], c)

    order = (2, 1, 3, 0)
    first = [[stage1("x", u, pl.ds(lo, hi - lo)) for u in order] for lo, hi in CHUNKS]
    second = [stage2("z", pl.ds(lo, hi - lo)) for lo, hi in CHUNKS]
    first_b = [stage1("z", u, cb) for u in order]
    second_b = stage2("x", cb)

    def home(ring, lo, hi):
        ring.arrive()
        for arr in (0, 1):
            v = ring.total(arr)
            if arr == 0:
                v = v * scale_s[:, :1]
            v = v.astype(BF)
            for i in range((hi - lo) // 128):
                tile = lo // 128 + i
                ex[tile // 8, arr, tile % 8] = v[:, 128 * i : 128 * (i + 1)]

    def exchange(k, e_to, e_from):
        return pltpu.make_async_remote_copy(
            src_ref=ex.at[k, e_to % 2, e_to // 2], dst_ref=rx.at[k, e_from],
            send_sem=xs.at[k, e_to], recv_sem=xr.at[k, e_from],
            device_id=(dp, e_to), device_id_type=MESH,
        )

    def exchange_start(k):
        def one(i, carry):
            exchange(k, (me + i) % NE, me).start()
            return carry

        lax.fori_loop(1, NE, one, 0)
        rx[k, me] = ex[k, core, slot]

    def place(k, owner):
        return out.at[
            owner % 2, :, pl.ds(pl.multiple_of(k * 1024 + (owner // 2) * 128, 128), 128)
        ]

    def spread(k, e_to, e_from):
        return pltpu.make_async_remote_copy(
            src_ref=ox.at[k], dst_ref=place(k, e_from),
            send_sem=os_.at[k, e_to], recv_sem=or_.at[k, e_from],
            device_id=(dp, e_to), device_id_type=MESH,
        )

    def keep(k):
        return pltpu.make_async_copy(ox.at[k], place(k, me), lsem.at[4 + k])

    def exchange_finish(k):
        def one(i, carry):
            exchange(k, me, (me + i) % NE).wait_recv()
            return carry

        lax.fori_loop(1, NE, one, 0)
        ox[k] = jnp.dot(
            sel_s[...], rx[k].reshape(NE * CAP, 128), preferred_element_type=F32
        ).astype(BF)
        keep(k).start()

        def two(i, carry):
            spread(k, (me + i) % NE, me).start()
            return carry

        lax.fori_loop(1, NE, two, 0)

    def grads(j):
        c = pl.ds(512 * j, 512)
        t = gat[:, :, 0, :, c].reshape(NE * CAP, 512)
        g = gat[:, :, 1, :, c].reshape(NE * CAP, 512)
        dg[:, c] = lax.dot_general(
            act_s[...].reshape(NE * CAP, HID), g, (((0,), (0,)), ((), ())),
            preferred_element_type=F32,
        ).astype(BF)
        gg[c, :] = lax.dot_general(
            t, gp_s[...].reshape(NE * CAP, HID), (((0,), (0,)), ((), ())),
            preferred_element_type=F32,
        ).astype(BF)

    for ring in first[0]:
        ring.start()
    for ring in first_b:
        ring.start()

    lo = lax.broadcasted_iota(jnp.int32, (NE, NE * CAP), 0) * CAP
    j = lax.broadcasted_iota(jnp.int32, (NE, NE * CAP), 1)
    ours = (j >= lo) & (j < lo + CAP)
    within = jnp.sum(jnp.where(ours, j - lo, 0), axis=0, keepdims=True).astype(F32)
    spread_e = jnp.where(ours, 1.0, 0.0).astype(BF)
    mem_x = jnp.dot(member.astype(BF), spread_e, preferred_element_type=F32)
    pos_x = jnp.dot(pos.astype(BF), spread_e, preferred_element_type=F32)
    sel_s[...] = jnp.where((mem_x > 0.5) & (pos_x == within), 1.0, 0.0).astype(BF)

    for k in range(NCH):
        for i in range(4):
            first[k][i].fwd()
            if k == 0:
                grads(i)
                first_b[i].fwd()
            if k + 1 < NCH:
                first[k + 1][i].start()
        if k == 0:
            grads(4)
            grads(5)
            store_gg = pltpu.make_async_copy(gg, gg_out, lsem.at[2])
            store_dg = pltpu.make_async_copy(dg, dg_out, lsem.at[3])
            store_gg.start()
            store_dg.start()
        for i in range(4):
            first[k][i].fin()
        second[k].start()
        if k == 0:
            for i in range(4):
                first_b[i].fin()
            second_b.start()
        if k >= 1:
            lo_c, hi_c = CHUNKS[k - 1]
            if k == 1:
                second_b.fwd()
            home(second[k - 1], lo_c, hi_c)
            exchange_start(k - 1)
        if k >= 2:
            exchange_finish(k - 2)
        second[k].fwd()
    home(second_b, A_COLS, D)
    home(second[NCH - 1], *CHUNKS[NCH - 1])
    exchange_start(NCH - 1)
    exchange_finish(NCH - 2)
    exchange_finish(NCH - 1)

    store_gg.wait()
    store_dg.wait()
    for k in range(NCH):
        keep(k).wait()

        def last(i, carry, k=k):
            spread(k, me, (me + i) % NE).wait_recv()
            spread(k, (me + i) % NE, me).wait_send()
            exchange(k, (me + i) % NE, me).wait_send()
            return carry

        lax.fori_loop(1, NE, last, 0)
    for copy in started:
        copy.wait_send()


N_COPY = 10 * 6 + 20 * 6


def shards(tokens, cotangent, routes, route_weights, gate_weight, down_weight):
    gate_weight = gate_weight.reshape(D, HID)
    down_weight = down_weight.reshape(HID, D)
    out, gg, dg = pl.pallas_call(
        kernel,
        out_shape=(
            jax.ShapeDtypeStruct((2, TOK, D), BF),
            jax.ShapeDtypeStruct((D, HID), BF),
            jax.ShapeDtypeStruct((HID, D), BF),
        ),
        in_specs=[VM, VM, VM, VM, HB, HB],
        out_specs=(HB, HB, HB),
        scratch_shapes=[
            pltpu.VMEM((4, 4, 2, CAP, D), BF),
            pltpu.VMEM((4, 4, 2, CAP, D), BF),
            pltpu.VMEM((4, 3, 2, CAP, D), BF),
            pltpu.VMEM((3, 2, CAP, D), BF),
            pltpu.VMEM((D, HID), BF),
            pltpu.VMEM((HID, D), BF),
            pltpu.VMEM((D, HID), BF),
            pltpu.VMEM((HID, D), BF),
            pltpu.VMEM((4, 4 * CAP, HID), BF),
            pltpu.VMEM((4, 4 * CAP, HID), BF),
            pltpu.VMEM((NCH, 2, 8, CAP, 128), BF),
            pltpu.VMEM((NCH, NE, CAP, 128), BF),
            pltpu.VMEM((NCH, TOK, 128), BF),
            pltpu.VMEM((TOK, NE * CAP), BF),
            pltpu.VMEM((CAP, 128), F32),
            pltpu.SemaphoreType.DMA((N_COPY,)),
            pltpu.SemaphoreType.DMA((N_COPY,)),
            pltpu.SemaphoreType.DMA((NCH, NE)),
            pltpu.SemaphoreType.DMA((NCH, NE)),
            pltpu.SemaphoreType.DMA((NCH, NE)),
            pltpu.SemaphoreType.DMA((NCH, NE)),
            pltpu.SemaphoreType.DMA((4 + NCH,)),
        ],
        compiler_params=pltpu.CompilerParams(
            collective_id=0, has_side_effects=True, vmem_limit_bytes=56 * 2**20
        ),
        cost_estimate=pl.CostEstimate(
            flops=12 * 768 * D * HID, bytes_accessed=2 * 10**7, transcendentals=768 * HID
        ),
        name="moe",
    )(tokens, cotangent, routes, route_weights, gate_weight, down_weight)
    return out[0], out[1], gg.reshape(1, D, HID), dg.reshape(1, HID, D)


def solution(mesh):
    return jax.shard_map(
        shards,
        mesh=mesh,
        in_specs=(
            P("dp", None),
            P("dp", None),
            P("dp", None),
            P("dp", None),
            P("expert", None, "dp"),
            P("expert", "dp", None),
        ),
        out_specs=(P("dp", None), P("dp", None), P("expert", None, "dp"), P("expert", "dp", None)),
        check_vma=False,
    )
```

time: 522 us -> 206 us (0.39)
  waiting for transfers between devices: 463 us -> 0 us
  Pallas kernels: 0 us -> 196 us
  matrix products: 38.5 us -> 0 us
  between operations: 13.9 us -> 0.65 us
    pallas_call x0 -> x1, Pallas kernels: none -> 196 us  [shards(): pl.pallas_call(kernel, out_shape=(jax.ShapeDtypeStruct((2, TOK, D), BF),...]
    reduce_scatter x2 -> x0, waiting for transfers between devices: 188 us -> none  [the longest x1 98.3 us: shards(): lax.psum_scatter(jnp.einsum('rlf,ldf->rld', piece, gate_weight, preferred...]
    all_gather x2 -> x0, waiting for transfers between devices: 159 us -> none  [the longest x1 84.5 us: shards(): token_rows = lax.all_gather(token_sel, 'dp', axis=0, tiled=True)]
    psum x1 -> x0, waiting for transfers between devices: 116 us -> none  [shards(): mixed = lax.psum(token_out.astype(jnp.bfloat16), 'expert')]
    dot_general x11 -> x0, matrix products: 38.5 us -> none  [the longest x1 6.55 us: shards(): jnp.einsum('rld,rlf->ldf', token_rows, grad_pre, preferred_element_type=j...]
  transfers between devices with their start and end apart: 5 -> 0, of which waited for: 5 -> 0; matrix products, arithmetic and copies ran while one was open for 7% -> 0% of each run, Pallas kernels for 0% -> 0%
where the time goes in v1:
time: 206 us
  Pallas kernels  196 us (95%)
  local copies, waits for them, and re-layouts  9.52 us (5%)
    pallas_call x1, Pallas kernels, shards(): pl.pallas_call(kernel, out_shape=(jax.ShapeDtypeStruct((2, TOK, D), BF),...  196 us
    unnamed x8, local copies, waits for them, and re-layouts  6.76 us

profile of v1, /device:TPU:1, one launch (start us, length us, event | category | flops | bytes accessed | tf_op | source)
XLA Modules:
  0.0 206.2 jit_solution(7028655753068677049)
XLA Ops:
  0.6 1.4 copy.10.routes
  2.0 1.4 copy.11.wts
  3.5 196.0 %moe.1 = (bf16[2,128,3072]{2,1,0:T(8,128)(2,1)}, bf16[3072,384]{1,0:T(8,128)(2,1)}, bf16[384,3072]{1,0:T(8,128)(2,1)}) custom-call(bf16[128,3072]{1,0:T(8,128)(2,1)} %tok.1, bf16[128,3072]{1,0:T(8,128)(2,1)} %cot.1, s32[128,4]{1,0:T(8,128)} %copy.10.routes, f32[128,4]{1,0:T(8,128)} %copy.11.wts, bf16[3072,384]{1,0:T(8,128)(2,1)} %bitcast.10, ...), custom_call_target="tpu_custom_call" | custom-call | flops 10871635968 | bytes 20000000 | tf_op jit(solution)/shard_map/moe/pallas_call | solution.py:434
  199.5 0.0 copy-start.1
  199.5 2.8 %slice_bitcast_fusion = (bf16[128,3072]{1,0:T(8,128)(2,1)}, bf16[128,3072]{1,0:T(8,128)(2,1)}) fusion(bf16[2,128,3072]{2,1,0:T(8,128)(2,1)} %get-tuple-element.7), kind=kLoop, calls=%fused_computation | loop fusion | bytes 3145728 | tf_op jit(solution)/shard_map/squeeze | solution.py:475
  202.2 0.0 copy-done.1
  202.3 0.0 copy-start
  202.3 1.4 copy.14
  203.7 1.1 copy-done
  204.8 1.4 copy.15
Async XLA Ops:
  199.5 2.8 %copy-start.1 = (bf16[3072,384]{1,0:T(8,128)(2,1)S(1)}, bf16[3072,384]{1,0:T(8,128)(2,1)}, u32[]{:S(2)}) copy-start(bf16[3072,384]{1,0:T(8,128)(2,1)} %get-tuple-element.8) | copy-start | bytes 7077892
  202.3 2.5 %copy-start = (bf16[384,3072]{1,0:T(8,128)(2,1)S(1)}, bf16[384,3072]{1,0:T(8,128)(2,1)}, u32[]{:S(2)}) copy-start(bf16[384,3072]{1,0:T(8,128)(2,1)} %get-tuple-element.9) | copy-start | bytes 7077892

commit v2 on v1

v2 whole, which is shorter than its diff:
```python
import functools

import jax
import jax.numpy as jnp
from jax import lax
from jax.experimental import pallas as pl
from jax.experimental.pallas import tpu as pltpu
from jax.sharding import PartitionSpec as P

MESH = pl.DeviceIdType.MESH
POS = (0, 1, 3, 2)
BF = jnp.bfloat16
F32 = jnp.float32
CAP = 48
TOK = 128
D = 3072
HID = 384
NE = 16
RA = 2688
EDGES = (0, 512, 1024, 1536, 2048, 2432, 2688)
NCH = 3
VM = pl.BlockSpec(memory_space=pltpu.VMEM)
HB = pl.BlockSpec(memory_space=pl.ANY)


def kernel(
    tok_in, cot_in, routes, wts, gate_in, down_in,
    out, gg_out, dg_out,
    tok, cot, raw, twin, gat, par, rd1, rd2, gate, down, gg, dg, act_s, gp_s, ex, rx, full, sel_s, scale_s,
    ssem, rsem, xs, xr, os_, or_, ks, kr, ts, tr, lsem,
):
    dp = lax.axis_index("dp")
    me = lax.axis_index("expert")
    h, x = dp // 4, dp % 4
    core, slot = me % 2, me // 2
    y, z_lo = me // 4, slot % 2

    def peer(axis, step):
        if axis == "x":
            return (h * 4 + (x + step + 4) % 4, me)
        if axis == "y":
            return (dp, (((y + step + 4) % 4) * 2 + z_lo) * 2 + core)
        return (((h + step + 4) % 4) * 4 + x, me)

    load_tok = pltpu.make_async_copy(tok_in, tok, lsem.at[4])
    load_cot = pltpu.make_async_copy(cot_in, cot, lsem.at[5])
    load_gate = pltpu.make_async_copy(gate_in, gate, lsem.at[0])
    load_down = pltpu.make_async_copy(down_in, down, lsem.at[1])
    half = pl.multiple_of(core * (D // 2), 128)
    load_raw = pltpu.make_async_copy(
        tok_in.at[:, pl.ds(pl.multiple_of(half + y * 384, 128), 384)],
        raw.at[0, 0, 0, pl.ds(0, TOK)],
        lsem.at[6 + 2 * NCH],
    )
    load_raw.start()
    load_tok.start()
    load_cot.start()
    load_gate.start()
    load_down.start()

    barrier = pltpu.get_barrier_semaphore()
    for axis in ("x", "z"):
        for step in (1, -1):
            pl.semaphore_signal(barrier, inc=1, device_id=peer(axis, step), device_id_type=MESH)

    def greet(i, carry):
        pl.semaphore_signal(barrier, inc=1, device_id=(dp, (me + i) % NE), device_id_type=MESH)
        return carry

    lax.fori_loop(1, NE, greet, 0)

    r = routes[...]
    w = wts[...]
    row16 = lax.broadcasted_iota(jnp.int32, (NE, TOK), 0)
    member = jnp.zeros((NE, TOK), F32)
    w_e = jnp.zeros((1, TOK), F32)
    for k in range(4):
        member = member + jnp.where(r[k : k + 1] == row16, 1.0, 0.0)
        w_e = w_e + jnp.where(r[k : k + 1] == me, w[k : k + 1], 0.0)
    before = lax.broadcasted_iota(jnp.int32, (TOK, TOK), 0) < lax.broadcasted_iota(
        jnp.int32, (TOK, TOK), 1
    )
    pos = jnp.dot(
        member.astype(BF), jnp.where(before, 1.0, 0.0).astype(BF), preferred_element_type=F32
    )
    slots = lax.broadcasted_iota(jnp.int32, (CAP, TOK), 0).astype(F32)

    def select(expert):
        mine = jnp.where(row16 == expert, 1.0, 0.0)
        mem_e = jnp.sum(member * mine, axis=0, keepdims=True)
        pos_e = jnp.sum(pos * mine, axis=0, keepdims=True)
        return jnp.where((pos_e == slots) & (mem_e > 0.5), 1.0, 0.0)

    sel = select(me)
    scale = jnp.sum(sel * w_e, axis=1, keepdims=True)
    scale_s[...] = jnp.broadcast_to(scale, (CAP, 128))
    sel_b = sel.astype(BF)
    pair = jnp.concatenate([sel, select(slot * 2 + 1 - core)], axis=0).astype(BF)
    for i in range(3):
        raw[0, 0, 0, TOK : TOK + 32, 128 * i : 128 * (i + 1)] = pair[32 * i : 32 * (i + 1)]
    load_cot.wait()
    gat[0, 0, 1] = (jnp.dot(sel_b, cot[...], preferred_element_type=F32) * scale).astype(BF)

    load_raw.wait()
    pl.semaphore_wait(barrier, 4 + NE - 1)

    started = []
    count = [0]

    def remote(src, dst, device):
        i = count[0]
        count[0] += 1
        copy = pltpu.make_async_remote_copy(
            src_ref=src, dst_ref=dst, send_sem=ssem.at[i], recv_sem=rsem.at[i],
            device_id=device, device_id_type=MESH,
        )
        return copy

    def go(copy):
        copy.start()
        started.append(copy)

    class Gather:
        def __init__(self, axis, at):
            self.plus, self.minus = peer(axis, 1), peer(axis, -1)
            self.at = at
            self.p, self.m, self.f = {}, {}, {}
            for arr in (0, 1):
                self.p[arr] = remote(at(0, arr), at(3, arr), self.plus)
                self.m[arr] = remote(at(0, arr), at(1, arr), self.minus)
            self.f[0] = remote(at(3, 0), at(2, 0), self.plus)
            self.f[1] = remote(at(1, 1), at(2, 1), self.minus)

        def start(self, arr):
            first, second = (self.p, self.m) if arr == 0 else (self.m, self.p)
            go(first[arr])
            go(second[arr])

        def fwd(self, arr):
            (self.p if arr == 0 else self.m)[arr].wait_recv()
            go(self.f[arr])

        def near(self, arr):
            (self.m if arr == 0 else self.p)[arr].wait_recv()

        def far(self, arr):
            self.f[arr].wait_recv()

    CHUNKS = tuple(zip(EDGES[:-1], EDGES[1:]))
    def cut(i):
        return pl.ds(i * (D // 2), D // 2)

    def piece(i):
        return pl.ds(i * 80, 80)

    a1 = Gather("z", lambda i, part: gat.at[i, 0, 1, :, cut(part)])
    a2 = [
        Gather("x", functools.partial(lambda u, i, part: gat.at[u, i, 1, :, cut(part)], u))
        for u in range(4)
    ]
    def sides(g):
        return slice(1, 3) if g == "s" else (0 if g == 0 else 3)

    c1 = Gather("z", lambda i, part: raw.at[0, POS[i], 0, piece(part)])
    c2 = {
        g: Gather("x", functools.partial(lambda g, i, part: raw.at[0, sides(g), POS[i], piece(part)], g))
        for g in (0, "s", 2)
    }
    cy = {
        (u, v): Gather(
            "y",
            functools.partial(
                lambda u, v, i, part: raw.at[i, sides(u), sides(v), pl.ds(64 * part, 64)], u, v
            ),
        )
        for u in (0, "s", 2)
        for v in (0, "s", 2)
        if (u, v) != (0, 0)
    }

    def sibling(u, v):
        return pltpu.make_async_remote_copy(
            src_ref=twin.at[u, v], dst_ref=gat.at[u, v, 0, :, pl.ds(half, D // 2)],
            send_sem=ts.at[4 * u + v], recv_sem=tr.at[4 * u + v],
            device_id=(dp, slot * 2 + 1 - core), device_id_type=MESH,
        )

    def from_sibling(u, v):
        other = pl.multiple_of((1 - core) * (D // 2), 128)
        return pltpu.make_async_remote_copy(
            src_ref=twin.at[u, v], dst_ref=gat.at[u, v, 0, :, pl.ds(other, D // 2)],
            send_sem=ts.at[4 * u + v], recv_sem=tr.at[4 * u + v],
            device_id=(dp, slot * 2 + 1 - core), device_id_type=MESH,
        )

    def pick(u, v):
        both = jnp.concatenate(
            [raw[0, POS[u], POS[v], TOK : TOK + 32, 128 * i : 128 * (i + 1)] for i in range(3)], axis=0
        )
        for r in range(4):
            res = jnp.dot(both, raw[r, POS[u], POS[v], :TOK], preferred_element_type=F32).astype(BF)
            c = ((y + r) % 4) * 384
            gat[u, v, 0, :, pl.ds(pl.multiple_of(half + c, 128), 384)] = res[:CAP]
            twin[u, v, :, pl.ds(pl.multiple_of(c, 128), 384)] = res[CAP:]
        sibling(u, v).start()

    def token_rows(u):
        for v in range(4):
            if (u, v) != (0, 0):
                from_sibling(u, v).wait_recv()

    def finish(ring):
        ring.near(0)
        ring.near(1)
        ring.far(0)
        ring.far(1)

    def rows(ref):
        return ref.reshape(4 * CAP, ref.shape[-1])

    def batch(u):
        t = rows(gat[u, :, 0])
        pre = jnp.dot(t, gate[...], preferred_element_type=F32)
        back = lax.dot_general(
            rows(gat[u, :, 1]), down[...], (((1,), (1,)), ((), ())), preferred_element_type=F32
        )
        s = jax.nn.sigmoid(pre)
        act = (pre * s).astype(BF)
        gp = (back * s * (1.0 + pre * (1.0 - s))).astype(BF)
        act_s[u] = act
        gp_s[u] = gp

        def cols(j, carry):
            c = pl.ds(pl.multiple_of(j * 512, 512), 512)
            o = jnp.dot(act_s[u], down[:, c], preferred_element_type=F32).astype(BF)
            par[u, :, 0, :, c] = o.reshape(4, CAP, 512)
            b = lax.dot_general(
                gp_s[u], gate[c, :], (((1,), (1,)), ((), ())), preferred_element_type=F32
            ).astype(BF)
            par[u, :, 1, :, c] = b.reshape(4, CAP, 512)
            return carry

        lax.fori_loop(0, D // 512, cols, 0)

    def drain():
        for copy in started:
            copy.wait_send()
    class Reduce:
        def __init__(self, axis, at, land, c):
            plus, minus = peer(axis, 1), peer(axis, -1)
            self.at, self.land, self.c = at, land, c
            self.f0 = remote(at(2, 0), land(0, 0), plus)
            self.f1 = remote(at(2, 1), land(0, 1), minus)
            self.l1 = remote(at(1, 1), land(1, 1), plus)
            self.r0 = remote(at(3, 0), land(2, 0), minus)
            self.l0 = remote(at(1, 0), land(1, 0), plus)
            self.r1 = remote(at(3, 1), land(2, 1), minus)

        def start(self):
            go(self.f0)
            go(self.f1)
            go(self.l1)
            go(self.r0)

        def fwd(self):
            for f, copy, i, arr in ((self.f0, self.l0, 1, 0), (self.f1, self.r1, 3, 1)):
                f.wait_recv()
                dst = self.at(i, arr)
                dst[...] = (dst[...].astype(F32) + self.land(0, arr)[...].astype(F32)).astype(BF)
                go(copy)

        def total(self, arr):
            return (
                self.at(0, arr)[...].astype(F32)
                + self.land(1, arr)[...].astype(F32)
                + self.land(2, arr)[...].astype(F32)
            )

        def arrive(self):
            for copy in (self.l1, self.r0, self.l0, self.r1):
                copy.wait_recv()

        def fin(self):
            self.arrive()
            for arr in (0, 1):
                self.at(0, arr)[...] = self.total(arr).astype(BF)

    def stage1(axis, u, c):
        if axis == "x":
            at = lambda i, arr: par.at[u, i, arr, :, c]
        else:
            at = lambda i, arr: par.at[i, u, arr, :, c]
        return Reduce(axis, at, lambda kind, arr: rd1.at[u, kind, arr, :, c], c)

    def stage2(axis, c):
        if axis == "x":
            at = lambda i, arr: par.at[0, i, arr, :, c]
        else:
            at = lambda i, arr: par.at[i, 0, arr, :, c]
        return Reduce(axis, at, lambda kind, arr: rd2.at[kind, arr, :, c], c)

    order = (0, 1, 3, 2)
    every = (slice(None),)
    first = [
        [stage1("x", u, pl.ds(lo, hi - lo)) for u in (every if lo else order)] for lo, hi in CHUNKS
    ]
    second = [stage2("z", pl.ds(lo, hi - lo)) for lo, hi in CHUNKS]
    rb = pl.ds(RA, D - RA)
    first_b = [stage1("z", u, rb) for u in every]
    second_b = stage2("x", rb)

    def home(ring, lo, hi):
        ring.arrive()
        for arr in (0, 1):
            v = ring.total(arr)
            if arr == 0:
                v = v * scale_s[:, :1]
            v = v.astype(BF)
            for i in range((hi - lo) // 128):
                tile = lo // 128 + i
                ex[tile // 8, arr, tile % 8] = v[:, 128 * i : 128 * (i + 1)]

    def exchange(k, e_to, e_from):
        return pltpu.make_async_remote_copy(
            src_ref=ex.at[k, e_to % 2, e_to // 2], dst_ref=rx.at[k, e_from],
            send_sem=xs.at[k, e_to], recv_sem=xr.at[k, e_from],
            device_id=(dp, e_to), device_id_type=MESH,
        )

    def exchange_start(k):
        def one(i, carry):
            exchange(k, (me + i) % NE, me).start()
            return carry

        lax.fori_loop(1, NE, one, 0)
        rx[k, me] = ex[k, core, slot]

    def tile(k, owner):
        return pl.ds(pl.multiple_of(k * 1024 + owner * 128, 128), 128)

    def spread(k, to, frm):
        place = full.at[core, :, tile(k, frm)]
        return pltpu.make_async_remote_copy(
            src_ref=place, dst_ref=place,
            send_sem=os_.at[k, to], recv_sem=or_.at[k, frm],
            device_id=(dp, to * 2 + core), device_id_type=MESH,
        )

    def mix(k):
        def one(i, carry):
            exchange(k, me, (me + i) % NE).wait_recv()
            return carry

        lax.fori_loop(1, NE, one, 0)
        full[core, :, tile(k, slot)] = lax.dot_general(
            sel_s[...], rx[k].reshape(NE * CAP, 128), (((0,), (0,)), ((), ())),
            preferred_element_type=F32,
        ).astype(BF)

        def two(i, carry):
            spread(k, (slot + i) % 8, slot).start()
            return carry

        lax.fori_loop(1, 8, two, 0)

    def relay(k):
        place = full.at[core, :, 1024 * k : 1024 * (k + 1)]
        return pltpu.make_async_remote_copy(
            src_ref=place, dst_ref=place, send_sem=ks.at[k], recv_sem=kr.at[k],
            device_id=(dp, slot * 2 + 1 - core), device_id_type=MESH,
        )

    def keep(k, arr, i):
        part = (arr, slice(None), slice(1024 * k, 1024 * (k + 1)))
        return pltpu.make_async_copy(full.at[part], out.at[part], lsem.at[6 + 2 * k + i])

    def relay_start(k):
        def one(i, carry):
            spread(k, slot, (slot + i) % 8).wait_recv()
            return carry

        lax.fori_loop(1, 8, one, 0)
        relay(k).start()
        keep(k, core, 0).start()

    def relay_finish(k):
        other = full.at[1 - core, :, 1024 * k : 1024 * (k + 1)]
        pltpu.make_async_remote_copy(
            src_ref=other, dst_ref=other, send_sem=ks.at[k], recv_sem=kr.at[k],
            device_id=(dp, slot * 2 + 1 - core), device_id_type=MESH,
        ).wait_recv()
        keep(k, 1 - core, 1).start()

    def grads(j):
        c = pl.ds(512 * j, 512)
        t = gat[:, :, 0, :, c].reshape(NE * CAP, 512)
        g = gat[:, :, 1, :, c].reshape(NE * CAP, 512)
        dg[:, c] = lax.dot_general(
            act_s[...].reshape(NE * CAP, HID), g, (((0,), (0,)), ((), ())),
            preferred_element_type=F32,
        ).astype(BF)
        gg[c, :] = lax.dot_general(
            t, gp_s[...].reshape(NE * CAP, HID), (((0,), (0,)), ((), ())),
            preferred_element_type=F32,
        ).astype(BF)

    def drain():
        for copy in started:
            copy.wait_send()

    def both(f):
        f(0)
        f(1)

    def begin(ring):
        both(ring.start)

    def onward(ring):
        both(ring.fwd)

    both(c1.start)
    begin(c2[0])
    both(a1.start)
    begin(a2[0])
    load_tok.wait()
    gat[0, 0, 0] = jnp.dot(sel_b, tok[...], preferred_element_type=F32).astype(BF)
    onward(c2[0])
    both(c2[0].near)
    begin(cy[0, "s"])
    onward(c1)
    both(c1.near)
    begin(c2["s"])
    begin(cy["s", 0])
    both(c2[0].far)
    begin(cy[0, 2])
    onward(cy[0, "s"])
    onward(a2[0])
    a1.fwd(0)
    a2[3].start(0)
    a1.fwd(1)
    a2[1].start(1)
    both(c1.far)
    begin(c2[2])
    onward(c2["s"])
    onward(cy["s", 0])
    onward(cy[0, 2])
    both(c2["s"].near)
    begin(cy["s", "s"])
    a1.near(0)
    a2[1].start(0)
    a1.near(1)
    a2[3].start(1)
    finish(cy[0, "s"])
    pick(0, 1)
    pick(0, 3)
    onward(c2[2])
    finish(cy[0, 2])
    pick(0, 2)
    a2[3].fwd(0)
    a2[1].fwd(1)
    both(c2["s"].far)
    begin(cy["s", 2])
    a1.far(0)
    a2[2].start(0)
    a1.far(1)
    a2[2].start(1)
    finish(a2[0])
    load_gate.wait()
    load_down.wait()
    token_rows(0)
    batch(0)
    onward(cy["s", "s"])
    begin(cy[2, 0])
    both(c2[2].near)
    begin(cy[2, "s"])
    finish(cy["s", 0])
    pick(1, 0)
    pick(3, 0)
    a2[1].fwd(0)
    a2[3].fwd(1)
    both(c2[2].far)
    begin(cy[2, 2])
    onward(cy["s", 2])
    onward(cy[2, 0])
    finish(cy["s", "s"])
    pick(1, 1)
    pick(1, 3)
    pick(3, 1)
    pick(3, 3)
    onward(cy[2, "s"])
    a2[2].fwd(0)
    a2[2].fwd(1)
    onward(cy[2, 2])
    finish(cy["s", 2])
    pick(1, 2)
    pick(3, 2)
    finish(a2[1])
    token_rows(1)
    batch(1)
    first[0][0].start()
    finish(a2[3])
    token_rows(3)
    batch(3)
    first[0][1].start()
    first[0][2].start()
    finish(cy[2, 0])
    pick(2, 0)
    finish(cy[2, "s"])
    pick(2, 1)
    pick(2, 3)
    finish(cy[2, 2])
    pick(2, 2)
    finish(a2[2])
    token_rows(2)
    batch(2)
    first[0][3].start()
    for ring in first_b:
        ring.start()
    for e in range(NE):
        sel_s[CAP * e : CAP * (e + 1), :] = jnp.where(
            (pos[e : e + 1] == slots) & (member[e : e + 1] > 0.5), 1.0, 0.0
        ).astype(BF)

    n = len(CHUNKS)
    ready = []
    todo = []

    def came(k):
        home(second[k], *CHUNKS[k])
        hi = CHUNKS[k][1]
        if hi in (1024, 2048, RA):
            g = {1024: 0, 2048: 1, RA: 2}[hi]
            if g == 2:
                home(second_b, RA, D)
            exchange_start(g)
            todo.append([g, 0])

    def advance():
        for item in todo:
            g, state = item
            if state < 3:
                (mix, relay_start, relay_finish)[state](g)
                item[1] += 1

    for k in range(n):
        for i, ring in enumerate(first[k]):
            ring.fwd()
            if k == 0:
                grads(i)
            if k + 1 < n and i == 0:
                first[k + 1][0].start()
        if k == 0:
            for ring in first_b:
                ring.fwd()
            grads(4)
            grads(5)
            store_gg = pltpu.make_async_copy(gg, gg_out, lsem.at[2])
            store_dg = pltpu.make_async_copy(dg, dg_out, lsem.at[3])
            store_gg.start()
            store_dg.start()
        if k >= 1:
            second[k - 1].fwd()
        if k >= 2:
            advance()
            came(k - 2)
        for ring in first[k]:
            ring.fin()
        second[k].start()
        if k == 1:
            for ring in first_b:
                ring.fin()
            second_b.start()
        if k == 2:
            second_b.fwd()
    advance()
    came(n - 2)
    second[n - 1].fwd()
    advance()
    came(n - 1)
    advance()
    advance()
    advance()

    store_gg.wait()
    store_dg.wait()
    for k in range(NCH):
        keep(k, core, 0).wait()
        keep(k, 1 - core, 1).wait()
        relay(k).wait_send()

        def last(i, carry, k=k):
            exchange(k, (me + i) % NE, me).wait_send()
            return carry

        lax.fori_loop(1, NE, last, 0)

        def last_spread(i, carry, k=k):
            spread(k, (slot + i) % 8, slot).wait_send()
            return carry

        lax.fori_loop(1, 8, last_spread, 0)
    for u in range(4):
        for v in range(4):
            if (u, v) != (0, 0):
                sibling(u, v).wait_send()
    drain()


N_COPY = 10 * 6 + 5 * 6 * len(EDGES)


def shards(tokens, cotangent, routes, route_weights, gate_weight, down_weight):
    gate_weight = gate_weight.reshape(D, HID)
    down_weight = down_weight.reshape(HID, D)
    out, gg, dg = pl.pallas_call(
        kernel,
        out_shape=(
            jax.ShapeDtypeStruct((2, TOK, D), BF),
            jax.ShapeDtypeStruct((D, HID), BF),
            jax.ShapeDtypeStruct((HID, D), BF),
        ),
        in_specs=[HB, HB, VM, VM, HB, HB],
        out_specs=(HB, HB, HB),
        scratch_shapes=[
            pltpu.VMEM((TOK, D), BF),
            pltpu.VMEM((TOK, D), BF),
            pltpu.VMEM((4, 4, 4, TOK + 32, 384), BF),
            pltpu.VMEM((4, 4, CAP, D // 2), BF),
            pltpu.VMEM((4, 4, 2, CAP, D), BF),
            pltpu.VMEM((4, 4, 2, CAP, D), BF),
            pltpu.VMEM((4, 3, 2, CAP, D), BF),
            pltpu.VMEM((3, 2, CAP, D), BF),
            pltpu.VMEM((D, HID), BF),
            pltpu.VMEM((HID, D), BF),
            pltpu.VMEM((D, HID), BF),
            pltpu.VMEM((HID, D), BF),
            pltpu.VMEM((4, 4 * CAP, HID), BF),
            pltpu.VMEM((4, 4 * CAP, HID), BF),
            pltpu.VMEM((NCH, 2, 8, CAP, 128), BF),
            pltpu.VMEM((NCH, NE, CAP, 128), BF),
            pltpu.VMEM((2, TOK, D), BF),
            pltpu.VMEM((NE * CAP, TOK), BF),
            pltpu.VMEM((CAP, 128), F32),
            pltpu.SemaphoreType.DMA((10 * 6 + 15 * 6 + 5 * 6 * len(EDGES),)),
            pltpu.SemaphoreType.DMA((10 * 6 + 15 * 6 + 5 * 6 * len(EDGES),)),
            pltpu.SemaphoreType.DMA((NCH, NE)),
            pltpu.SemaphoreType.DMA((NCH, NE)),
            pltpu.SemaphoreType.DMA((NCH, 8)),
            pltpu.SemaphoreType.DMA((NCH, 8)),
            pltpu.SemaphoreType.DMA((NCH,)),
            pltpu.SemaphoreType.DMA((NCH,)),
            pltpu.SemaphoreType.DMA((16,)),
            pltpu.SemaphoreType.DMA((16,)),
            pltpu.SemaphoreType.DMA((7 + 2 * NCH,)),
        ],
        compiler_params=pltpu.CompilerParams(
            collective_id=0, has_side_effects=True, vmem_limit_bytes=60 * 2**20
        ),
        cost_estimate=pl.CostEstimate(
            flops=12 * 768 * D * HID, bytes_accessed=2 * 10**7, transcendentals=768 * HID
        ),
        name="moe",
    )(tokens, cotangent, routes.T, route_weights.T, gate_weight, down_weight)
    return out[0], out[1], gg.reshape(1, D, HID), dg.reshape(1, HID, D)


def solution(mesh):
    return jax.shard_map(
        shards,
        mesh=mesh,
        in_specs=(
            P("dp", None),
            P("dp", None),
            P("dp", None),
            P("dp", None),
            P("expert", None, "dp"),
            P("expert", "dp", None),
        ),
        out_specs=(P("dp", None), P("dp", None), P("expert", None, "dp"), P("expert", "dp", None)),
        check_vma=False,
    )
```

time: 206 us -> 194 us (0.942)
  Pallas kernels: 196 us -> 186 us
  local copies, waits for them, and re-layouts: 9.52 us -> 6.69 us
    pallas_call x1, Pallas kernels: 196 us -> 186 us  [shards(): pl.pallas_call(kernel, out_shape=(jax.ShapeDtypeStruct((2, TOK, D), BF),...]
    unnamed x8 -> x6, local copies, waits for them, and re-layouts: 6.76 us -> 3.93 us
where the time goes in v2:
time: 194 us
  Pallas kernels  186 us (96%)
  local copies, waits for them, and re-layouts  6.69 us (3%)
    pallas_call x1, Pallas kernels, shards(): pl.pallas_call(kernel, out_shape=(jax.ShapeDtypeStruct((2, TOK, D), BF),...  186 us
    unnamed x6, local copies, waits for them, and re-layouts  3.93 us

profile of v2, /device:TPU:1, one launch (start us, length us, event | category | flops | bytes accessed | tf_op | source)
XLA Modules:
  0.0 193.7 jit_solution(18062325673261594955)
XLA Ops:
  0.6 186.4 %moe.1 = (bf16[2,128,3072]{2,1,0:T(8,128)(2,1)}, bf16[3072,384]{1,0:T(8,128)(2,1)}, bf16[384,3072]{1,0:T(8,128)(2,1)}) custom-call(bf16[128,3072]{1,0:T(8,128)(2,1)} %tok_in.1, bf16[128,3072]{1,0:T(8,128)(2,1)} %cot_in.1, s32[4,128]{1,0:T(4,128)} %bitcast.14, f32[4,128]{1,0:T(4,128)} %bitcast.15, bf16[3072,384]{1,0:T(8,128)(2,1)} %bitcast.12, ...), custom_call_target="tpu_custom_call" | custom-call | flops 10871635968 | bytes 20000000 | tf_op jit(solution)/shard_map/moe/pallas_call | solution.py:615
  187.0 0.0 copy-start.1
  187.0 2.8 %slice_bitcast_fusion = (bf16[128,3072]{1,0:T(8,128)(2,1)}, bf16[128,3072]{1,0:T(8,128)(2,1)}) fusion(bf16[2,128,3072]{2,1,0:T(8,128)(2,1)} %get-tuple-element.7), kind=kLoop, calls=%fused_computation | loop fusion | bytes 3145728 | tf_op jit(solution)/shard_map/squeeze | solution.py:664
  189.8 0.0 copy-done.1
  189.8 0.0 copy-start
  189.8 1.4 copy.12
  191.2 1.1 copy-done
  192.3 1.4 copy.13
Async XLA Ops:
  187.0 2.8 %copy-start.1 = (bf16[3072,384]{1,0:T(8,128)(2,1)S(1)}, bf16[3072,384]{1,0:T(8,128)(2,1)}, u32[]{:S(2)}) copy-start(bf16[3072,384]{1,0:T(8,128)(2,1)} %get-tuple-element.8) | copy-start | bytes 7077892
  189.8 2.5 %copy-start = (bf16[384,3072]{1,0:T(8,128)(2,1)S(1)}, bf16[384,3072]{1,0:T(8,128)(2,1)}, u32[]{:S(2)}) copy-start(bf16[384,3072]{1,0:T(8,128)(2,1)} %get-tuple-element.9) | copy-start | bytes 7077892

commit v3 on v2

--- a/solution.py
+++ b/solution.py
@@ -25,7 +25,7 @@
 
 def kernel(
     tok_in, cot_in, routes, wts, gate_in, down_in,
-    out, gg_out, dg_out,
+    mixed, tgrad, gg_out, dg_out,
     tok, cot, raw, twin, gat, par, rd1, rd2, gate, down, gg, dg, act_s, gp_s, ex, rx, full, sel_s, scale_s,
     ssem, rsem, xs, xr, os_, or_, ks, kr, ts, tr, lsem,
 ):
@@ -242,9 +242,11 @@
 
         lax.fori_loop(0, D // 512, cols, 0)
 
-    def drain():
-        for copy in started:
-            copy.wait_send()
+    def drain(upto):
+        for copy in started[:upto]:
+            if copy is not None:
+                copy.wait_send()
+        started[:upto] = [None] * upto
     class Reduce:
         def __init__(self, axis, at, land, c):
             plus, minus = peer(axis, 1), peer(axis, -1)
@@ -306,8 +308,11 @@
     ]
     second = [stage2("z", pl.ds(lo, hi - lo)) for lo, hi in CHUNKS]
     rb = pl.ds(RA, D - RA)
-    first_b = [stage1("z", u, rb) for u in every]
-    second_b = stage2("x", rb)
+    if RA < D:
+        first_b = [stage1("z", u, rb) for u in every]
+        second_b = stage2("x", rb)
+    else:
+        first_b = []
 
     def home(ring, lo, hi):
         ring.arrive()
@@ -370,9 +375,11 @@
             device_id=(dp, slot * 2 + 1 - core), device_id_type=MESH,
         )
 
-    def keep(k, arr, i):
-        part = (arr, slice(None), slice(1024 * k, 1024 * (k + 1)))
-        return pltpu.make_async_copy(full.at[part], out.at[part], lsem.at[6 + 2 * k + i])
+    def keep(k, arr):
+        cols = slice(1024 * k, 1024 * (k + 1))
+        return pltpu.make_async_copy(
+            full.at[arr, :, cols], (mixed, tgrad)[arr].at[:, cols], lsem.at[6 + 2 * k + arr]
+        )
 
     def relay_start(k):
         def one(i, carry):
@@ -381,7 +388,6 @@
 
         lax.fori_loop(1, 8, one, 0)
         relay(k).start()
-        keep(k, core, 0).start()
 
     def relay_finish(k):
         other = full.at[1 - core, :, 1024 * k : 1024 * (k + 1)]
@@ -389,7 +395,8 @@
             src_ref=other, dst_ref=other, send_sem=ks.at[k], recv_sem=kr.at[k],
             device_id=(dp, slot * 2 + 1 - core), device_id_type=MESH,
         ).wait_recv()
-        keep(k, 1 - core, 1).start()
+        keep(k, 0).start()
+        keep(k, 1).start()
 
     def grads(j):
         c = pl.ds(512 * j, 512)
@@ -404,9 +411,11 @@
             preferred_element_type=F32,
         ).astype(BF)
 
-    def drain():
-        for copy in started:
-            copy.wait_send()
+    def drain(upto):
+        for copy in started[:upto]:
+            if copy is not None:
+                copy.wait_send()
+        started[:upto] = [None] * upto
 
     def both(f):
         f(0)
@@ -420,7 +429,6 @@
 
     both(c1.start)
     begin(c2[0])
-    both(a1.start)
     begin(a2[0])
     load_tok.wait()
     gat[0, 0, 0] = jnp.dot(sel_b, tok[...], preferred_element_type=F32).astype(BF)
@@ -428,24 +436,25 @@
     both(c2[0].near)
     begin(cy[0, "s"])
     onward(c1)
+    both(a1.start)
     both(c1.near)
     begin(c2["s"])
     begin(cy["s", 0])
     both(c2[0].far)
     begin(cy[0, 2])
+    both(c1.far)
+    begin(c2[2])
     onward(cy[0, "s"])
     onward(a2[0])
-    a1.fwd(0)
-    a2[3].start(0)
-    a1.fwd(1)
-    a2[1].start(1)
-    both(c1.far)
-    begin(c2[2])
     onward(c2["s"])
     onward(cy["s", 0])
     onward(cy[0, 2])
     both(c2["s"].near)
     begin(cy["s", "s"])
+    a1.fwd(0)
+    a2[3].start(0)
+    a1.fwd(1)
+    a2[1].start(1)
     a1.near(0)
     a2[1].start(0)
     a1.near(1)
@@ -470,41 +479,41 @@
     token_rows(0)
     batch(0)
     onward(cy["s", "s"])
-    begin(cy[2, 0])
-    both(c2[2].near)
-    begin(cy[2, "s"])
     finish(cy["s", 0])
     pick(1, 0)
     pick(3, 0)
     a2[1].fwd(0)
     a2[3].fwd(1)
-    both(c2[2].far)
-    begin(cy[2, 2])
     onward(cy["s", 2])
-    onward(cy[2, 0])
+    both(c2[2].near)
+    begin(cy[2, 0])
+    begin(cy[2, "s"])
     finish(cy["s", "s"])
     pick(1, 1)
     pick(1, 3)
+    both(c2[2].far)
+    begin(cy[2, 2])
     pick(3, 1)
     pick(3, 3)
-    onward(cy[2, "s"])
     a2[2].fwd(0)
     a2[2].fwd(1)
-    onward(cy[2, 2])
     finish(cy["s", 2])
     pick(1, 2)
     pick(3, 2)
+    onward(cy[2, 0])
+    onward(cy[2, "s"])
     finish(a2[1])
     token_rows(1)
     batch(1)
     first[0][0].start()
+    onward(cy[2, 2])
+    finish(cy[2, 0])
+    pick(2, 0)
     finish(a2[3])
     token_rows(3)
     batch(3)
     first[0][1].start()
     first[0][2].start()
-    finish(cy[2, 0])
-    pick(2, 0)
     finish(cy[2, "s"])
     pick(2, 1)
     pick(2, 3)
@@ -531,7 +540,8 @@
         if hi in (1024, 2048, RA):
             g = {1024: 0, 2048: 1, RA: 2}[hi]
             if g == 2:
-                home(second_b, RA, D)
+                if RA < D:
+                    home(second_b, RA, D)
             exchange_start(g)
             todo.append([g, 0])
 
@@ -543,15 +553,17 @@
                 item[1] += 1
 
     for k in range(n):
+        mark = len(started)
         for i, ring in enumerate(first[k]):
             ring.fwd()
             if k == 0:
                 grads(i)
             if k + 1 < n and i == 0:
                 first[k + 1][0].start()
-        if k == 0:
+        if k == 1:
             for ring in first_b:
                 ring.fwd()
+        if k == 0:
             grads(4)
             grads(5)
             store_gg = pltpu.make_async_copy(gg, gg_out, lsem.at[2])
@@ -563,29 +575,34 @@
         if k >= 2:
             advance()
             came(k - 2)
+            drain(old)
+        old = mark
         for ring in first[k]:
             ring.fin()
         second[k].start()
-        if k == 1:
+        if k == 2 and RA < D:
             for ring in first_b:
                 ring.fin()
             second_b.start()
-        if k == 2:
+        if k == 3 and RA < D:
             second_b.fwd()
-    advance()
     came(n - 2)
     second[n - 1].fwd()
-    advance()
     came(n - 1)
-    advance()
-    advance()
-    advance()
+    mix(1)
+    relay_finish(0)
+    mix(2)
+    relay_start(1)
+    drain(old)
+    relay_start(2)
+    relay_finish(1)
+    relay_finish(2)
 
     store_gg.wait()
     store_dg.wait()
     for k in range(NCH):
-        keep(k, core, 0).wait()
-        keep(k, 1 - core, 1).wait()
+        keep(k, 0).wait()
+        keep(k, 1).wait()
         relay(k).wait_send()
 
         def last(i, carry, k=k):
@@ -603,7 +620,7 @@
         for v in range(4):
             if (u, v) != (0, 0):
                 sibling(u, v).wait_send()
-    drain()
+    drain(len(started))
 
 
 N_COPY = 10 * 6 + 5 * 6 * len(EDGES)
@@ -612,15 +629,16 @@
 def shards(tokens, cotangent, routes, route_weights, gate_weight, down_weight):
     gate_weight = gate_weight.reshape(D, HID)
     down_weight = down_weight.reshape(HID, D)
-    out, gg, dg = pl.pallas_call(
+    mixed, tgrad, gg, dg = pl.pallas_call(
         kernel,
         out_shape=(
-            jax.ShapeDtypeStruct((2, TOK, D), BF),
+            jax.ShapeDtypeStruct((TOK, D), BF),
+            jax.ShapeDtypeStruct((TOK, D), BF),
             jax.ShapeDtypeStruct((D, HID), BF),
             jax.ShapeDtypeStruct((HID, D), BF),
         ),
         in_specs=[HB, HB, VM, VM, HB, HB],
-        out_specs=(HB, HB, HB),
+        out_specs=(HB, HB, HB, HB),
         scratch_shapes=[
             pltpu.VMEM((TOK, D), BF),
             pltpu.VMEM((TOK, D), BF),
@@ -661,7 +679,7 @@
         ),
         name="moe",
     )(tokens, cotangent, routes.T, route_weights.T, gate_weight, down_weight)
-    return out[0], out[1], gg.reshape(1, D, HID), dg.reshape(1, HID, D)
+    return mixed, tgrad, gg.reshape(1, D, HID), dg.reshape(1, HID, D)
 
 
 def solution(mesh):

time: 194 us -> 187 us (0.964)
  Pallas kernels: 186 us -> 177 us
    pallas_call x1, Pallas kernels: 186 us -> 177 us  [shards(): pl.pallas_call(kernel, out_shape=(jax.ShapeDtypeStruct((TOK, D), BF), jax...]
    unnamed x6 -> x8, local copies, waits for them, and re-layouts: 3.93 us -> 8.2 us
    squeeze x1 -> x0, local copies, waits for them, and re-layouts: 2.76 us -> none  [shards(): return (out[0], out[1], gg.reshape(1, D, HID), dg.reshape(1, HID, D))]
where the time goes in v3:
time: 187 us; the launch traced here: 186 us
  Pallas kernels  177 us (95%)
  local copies, waits for them, and re-layouts  8.2 us (4%)
    pallas_call x1, Pallas kernels, shards(): pl.pallas_call(kernel, out_shape=(jax.ShapeDtypeStruct((TOK, D), BF), jax...  177 us
    unnamed x8, local copies, waits for them, and re-layouts  8.2 us

profile of v3, /device:TPU:1, one launch (start us, length us, event | category | flops | bytes accessed | tf_op | source)
XLA Modules:
  0.0 186.3 jit_solution(7078628840944014182)
XLA Ops:
  0.6 177.5 %moe.1 = (bf16[128,3072]{1,0:T(8,128)(2,1)}, bf16[128,3072]{1,0:T(8,128)(2,1)}, bf16[3072,384]{1,0:T(8,128)(2,1)}, bf16[384,3072]{1,0:T(8,128)(2,1)}) custom-call(bf16[128,3072]{1,0:T(8,128)(2,1)} %tok_in.1, bf16[128,3072]{1,0:T(8,128)(2,1)} %cot_in.1, s32[4,128]{1,0:T(4,128)} %bitcast.10, f32[4,128]{1,0:T(4,128)} %bitcast.11, bf16[3072,384]{1,0:T(8,128)(2,1)} %bitcast.8, ...), custom_call_target="tpu_custom_call" | custom-call | flops 10871635968 | bytes 20000000 | tf_op jit(solution)/shard_map/moe/pallas_call | solution.py:632
  178.1 0.0 copy-start.1
  178.1 2.2 %copy.14 = bf16[128,3072]{1,0:T(8,128)(2,1)} copy(bf16[128,3072]{1,0:T(8,128)(2,1)} %get-tuple-element.16) | data formatting | bytes 1572864
  180.3 2.1 %copy.15 = bf16[128,3072]{1,0:T(8,128)(2,1)} copy(bf16[128,3072]{1,0:T(8,128)(2,1)} %get-tuple-element.17) | data formatting | bytes 1572864
  182.4 0.0 copy-done.1
  182.4 0.0 copy-start
  182.4 1.4 copy.16
  183.8 1.1 copy-done
  184.9 1.4 copy.17
Async XLA Ops:
  178.1 4.3 %copy-start.1 = (bf16[3072,384]{1,0:T(8,128)(2,1)S(1)}, bf16[3072,384]{1,0:T(8,128)(2,1)}, u32[]{:S(2)}) copy-start(bf16[3072,384]{1,0:T(8,128)(2,1)} %get-tuple-element.10) | copy-start | bytes 7077892
  182.4 2.5 %copy-start = (bf16[384,3072]{1,0:T(8,128)(2,1)S(1)}, bf16[384,3072]{1,0:T(8,128)(2,1)}, u32[]{:S(2)}) copy-start(bf16[384,3072]{1,0:T(8,128)(2,1)} %get-tuple-element.11) | copy-start | bytes 7077892

commit v4 on v3

--- a/solution.py
+++ b/solution.py
@@ -16,8 +16,9 @@
 D = 3072
 HID = 384
 NE = 16
-RA = 2688
-EDGES = (0, 512, 1024, 1536, 2048, 2432, 2688)
+RA = 2560
+GA = 2304
+EDGES = (0, 512, 1024, 1536, 2048, 2304, 2560)
 NCH = 3
 VM = pl.BlockSpec(memory_space=pltpu.VMEM)
 HB = pl.BlockSpec(memory_space=pl.ANY)
@@ -25,8 +26,8 @@
 
 def kernel(
     tok_in, cot_in, routes, wts, gate_in, down_in,
-    mixed, tgrad, gg_out, dg_out,
-    tok, cot, raw, twin, gat, par, rd1, rd2, gate, down, gg, dg, act_s, gp_s, ex, rx, full, sel_s, scale_s,
+    mixed, tgrad, gg, dg,
+    tok, cot, raw, twin, gat, par, rd1, rd2, gate, down, act_s, gp_s, ex, rx, full, sel_s, scale_s,
     ssem, rsem, xs, xr, os_, or_, ks, kr, ts, tr, lsem,
 ):
     dp = lax.axis_index("dp")
@@ -98,9 +99,6 @@
     pair = jnp.concatenate([sel, select(slot * 2 + 1 - core)], axis=0).astype(BF)
     for i in range(3):
         raw[0, 0, 0, TOK : TOK + 32, 128 * i : 128 * (i + 1)] = pair[32 * i : 32 * (i + 1)]
-    load_cot.wait()
-    gat[0, 0, 1] = (jnp.dot(sel_b, cot[...], preferred_element_type=F32) * scale).astype(BF)
-
     load_raw.wait()
     pl.semaphore_wait(barrier, 4 + NE - 1)
 
@@ -148,7 +146,10 @@
 
     CHUNKS = tuple(zip(EDGES[:-1], EDGES[1:]))
     def cut(i):
-        return pl.ds(i * (D // 2), D // 2)
+        return pl.ds(i * (GA // 2), GA // 2)
+
+    def rest(i):
+        return pl.ds(GA + i * ((D - GA) // 2), (D - GA) // 2)
 
     def piece(i):
         return pl.ds(i * 80, 80)
@@ -161,6 +162,11 @@
     def sides(g):
         return slice(1, 3) if g == "s" else (0 if g == 0 else 3)
 
+    b1 = Gather("x", lambda i, part: gat.at[0, i, 1, :, rest(part)])
+    b2 = [
+        Gather("z", functools.partial(lambda u, i, part: gat.at[i, u, 1, :, rest(part)], u))
+        for u in range(4)
+    ]
     c1 = Gather("z", lambda i, part: raw.at[0, POS[i], 0, piece(part)])
     c2 = {
         g: Gather("x", functools.partial(lambda g, i, part: raw.at[0, sides(g), POS[i], piece(part)], g))
@@ -429,6 +435,9 @@
 
     both(c1.start)
     begin(c2[0])
+    load_cot.wait()
+    gat[0, 0, 1] = (jnp.dot(sel_b, cot[...], preferred_element_type=F32) * scale).astype(BF)
+    begin(b1)
     begin(a2[0])
     load_tok.wait()
     gat[0, 0, 0] = jnp.dot(sel_b, tok[...], preferred_element_type=F32).astype(BF)
@@ -445,6 +454,8 @@
     both(c1.far)
     begin(c2[2])
     onward(cy[0, "s"])
+    onward(b1)
+    begin(b2[0])
     onward(a2[0])
     onward(c2["s"])
     onward(cy["s", 0])
@@ -473,6 +484,12 @@
     a2[2].start(0)
     a1.far(1)
     a2[2].start(1)
+    both(b1.near)
+    begin(b2[1])
+    begin(b2[3])
+    onward(b2[0])
+    both(b1.far)
+    begin(b2[2])
     finish(a2[0])
     load_gate.wait()
     load_down.wait()
@@ -485,6 +502,8 @@
     a2[1].fwd(0)
     a2[3].fwd(1)
     onward(cy["s", 2])
+    onward(b2[1])
+    onward(b2[3])
     both(c2[2].near)
     begin(cy[2, 0])
     begin(cy[2, "s"])
@@ -495,6 +514,7 @@
     begin(cy[2, 2])
     pick(3, 1)
     pick(3, 3)
+    onward(b2[2])
     a2[2].fwd(0)
     a2[2].fwd(1)
     finish(cy["s", 2])
@@ -502,6 +522,8 @@
     pick(3, 2)
     onward(cy[2, 0])
     onward(cy[2, "s"])
+    for ring in b2:
+        both(ring.near)
     finish(a2[1])
     token_rows(1)
     batch(1)
@@ -519,6 +541,8 @@
     pick(2, 3)
     finish(cy[2, 2])
     pick(2, 2)
+    for ring in b2:
+        both(ring.far)
     finish(a2[2])
     token_rows(2)
     batch(2)
@@ -566,10 +590,6 @@
         if k == 0:
             grads(4)
             grads(5)
-            store_gg = pltpu.make_async_copy(gg, gg_out, lsem.at[2])
-            store_dg = pltpu.make_async_copy(dg, dg_out, lsem.at[3])
-            store_gg.start()
-            store_dg.start()
         if k >= 1:
             second[k - 1].fwd()
         if k >= 2:
@@ -598,8 +618,6 @@
     relay_finish(1)
     relay_finish(2)
 
-    store_gg.wait()
-    store_dg.wait()
     for k in range(NCH):
         keep(k, 0).wait()
         keep(k, 1).wait()
@@ -632,13 +650,13 @@
     mixed, tgrad, gg, dg = pl.pallas_call(
         kernel,
         out_shape=(
-            jax.ShapeDtypeStruct((TOK, D), BF),
-            jax.ShapeDtypeStruct((TOK, D), BF),
-            jax.ShapeDtypeStruct((D, HID), BF),
-            jax.ShapeDtypeStruct((HID, D), BF),
+            pltpu.VMEM((TOK, D), BF),
+            pltpu.VMEM((TOK, D), BF),
+            pltpu.VMEM((D, HID), BF),
+            pltpu.VMEM((HID, D), BF),
         ),
         in_specs=[HB, HB, VM, VM, HB, HB],
-        out_specs=(HB, HB, HB, HB),
+        out_specs=(VM, VM, VM, VM),
         scratch_shapes=[
             pltpu.VMEM((TOK, D), BF),
             pltpu.VMEM((TOK, D), BF),
@@ -650,8 +668,6 @@
             pltpu.VMEM((3, 2, CAP, D), BF),
             pltpu.VMEM((D, HID), BF),
             pltpu.VMEM((HID, D), BF),
-            pltpu.VMEM((D, HID), BF),
-            pltpu.VMEM((HID, D), BF),
             pltpu.VMEM((4, 4 * CAP, HID), BF),
             pltpu.VMEM((4, 4 * CAP, HID), BF),
             pltpu.VMEM((NCH, 2, 8, CAP, 128), BF),
@@ -659,8 +675,8 @@
             pltpu.VMEM((2, TOK, D), BF),
             pltpu.VMEM((NE * CAP, TOK), BF),
             pltpu.VMEM((CAP, 128), F32),
-            pltpu.SemaphoreType.DMA((10 * 6 + 15 * 6 + 5 * 6 * len(EDGES),)),
-            pltpu.SemaphoreType.DMA((10 * 6 + 15 * 6 + 5 * 6 * len(EDGES),)),
+            pltpu.SemaphoreType.DMA((15 * 6 + 15 * 6 + 5 * 6 * len(EDGES),)),
+            pltpu.SemaphoreType.DMA((15 * 6 + 15 * 6 + 5 * 6 * len(EDGES),)),
             pltpu.SemaphoreType.DMA((NCH, NE)),
             pltpu.SemaphoreType.DMA((NCH, NE)),
             pltpu.SemaphoreType.DMA((NCH, 8)),
@@ -672,7 +688,7 @@
             pltpu.SemaphoreType.DMA((7 + 2 * NCH,)),
         ],
         compiler_params=pltpu.CompilerParams(
-            collective_id=0, has_side_effects=True, vmem_limit_bytes=60 * 2**20
+            collective_id=0, has_side_effects=True, vmem_limit_bytes=56 * 2**20
         ),
         cost_estimate=pl.CostEstimate(
             flops=12 * 768 * D * HID, bytes_accessed=2 * 10**7, transcendentals=768 * HID

time: 187 us -> 180 us (0.963)
  local copies, waits for them, and re-layouts: 8.2 us -> 4.57 us
  Pallas kernels: 177 us -> 175 us
    unnamed x8 -> x4, local copies, waits for them, and re-layouts: 8.2 us -> 4.57 us
    pallas_call x1, Pallas kernels: 177 us -> 175 us  [shards(): pl.pallas_call(kernel, out_shape=(pltpu.VMEM((TOK, D), BF), pltpu.VMEM((T...]
where the time goes in v4:
time: 180 us
  Pallas kernels  175 us (97%)
  local copies, waits for them, and re-layouts  4.57 us (3%)
    pallas_call x1, Pallas kernels, shards(): pl.pallas_call(kernel, out_shape=(pltpu.VMEM((TOK, D), BF), pltpu.VMEM((T...  175 us
    unnamed x4, local copies, waits for them, and re-layouts  4.57 us

profile of v4, /device:TPU:1, one launch (start us, length us, event | category | flops | bytes accessed | tf_op | source)
XLA Modules:
  0.0 179.9 jit_solution(8244737395407689516)
XLA Ops:
  0.6 174.7 %moe.1 = (bf16[128,3072]{1,0:T(8,128)(2,1)S(1)}, bf16[128,3072]{1,0:T(8,128)(2,1)S(1)}, bf16[3072,384]{1,0:T(8,128)(2,1)S(1)}, bf16[384,3072]{1,0:T(8,128)(2,1)S(1)}) custom-call(bf16[128,3072]{1,0:T(8,128)(2,1)} %tok_in.1, bf16[128,3072]{1,0:T(8,128)(2,1)} %cot_in.1, s32[4,128]{1,0:T(4,128)} %bitcast.10, f32[4,128]{1,0:T(4,128)} %bitcast.11, ...), custom_call_target="tpu_custom_call" | custom-call | flops 10871635968 | bytes 20000000 | tf_op jit(solution)/shard_map/moe/pallas_call | solution.py:650
  175.4 0.9 copy.14
  176.3 0.9 copy.15
  177.1 1.4 copy.16
  178.5 1.4 copy.17

commit v5 on v4

--- a/solution.py
+++ b/solution.py
@@ -490,11 +490,6 @@
     onward(b2[0])
     both(b1.far)
     begin(b2[2])
-    finish(a2[0])
-    load_gate.wait()
-    load_down.wait()
-    token_rows(0)
-    batch(0)
     onward(cy["s", "s"])
     finish(cy["s", 0])
     pick(1, 0)
@@ -507,6 +502,11 @@
     both(c2[2].near)
     begin(cy[2, 0])
     begin(cy[2, "s"])
+    finish(a2[0])
+    load_gate.wait()
+    load_down.wait()
+    token_rows(0)
+    batch(0)
     finish(cy["s", "s"])
     pick(1, 1)
     pick(1, 3)

time: 180 us -> 180 us (level)
  no operation moved by 1% of the time
where the time goes in v5:
time: 180 us
  Pallas kernels  175 us (97%)
  local copies, waits for them, and re-layouts  4.57 us (3%)
    pallas_call x1, Pallas kernels, shards(): pl.pallas_call(kernel, out_shape=(pltpu.VMEM((TOK, D), BF), pltpu.VMEM((T...  175 us
    unnamed x4, local copies, waits for them, and re-layouts  4.57 us

profile of v5, /device:TPU:1, one launch (start us, length us, event | category | flops | bytes accessed | tf_op | source)
XLA Modules:
  0.0 180.0 jit_solution(2493311404368804891)
XLA Ops:
  0.6 174.7 %moe.1 = (bf16[128,3072]{1,0:T(8,128)(2,1)S(1)}, bf16[128,3072]{1,0:T(8,128)(2,1)S(1)}, bf16[3072,384]{1,0:T(8,128)(2,1)S(1)}, bf16[384,3072]{1,0:T(8,128)(2,1)S(1)}) custom-call(bf16[128,3072]{1,0:T(8,128)(2,1)} %tok_in.1, bf16[128,3072]{1,0:T(8,128)(2,1)} %cot_in.1, s32[4,128]{1,0:T(4,128)} %bitcast.10, f32[4,128]{1,0:T(4,128)} %bitcast.11, ...), custom_call_target="tpu_custom_call" | custom-call | flops 10871635968 | bytes 20000000 | tf_op jit(solution)/shard_map/moe/pallas_call | solution.py:650
  175.4 0.9 copy.14
  176.3 0.9 copy.15
  177.1 1.4 copy.16
  178.6 1.4 copy.17
